TPU v7x, 32 devices: a whole 2x2x4 slice. The times are simulated.
32 devices in a mesh: blk: 8 (over z, x), sub: 4 (over y, core).
Axes of the slice: x: 2, y: 2, z: 4, core: 2. Of those that a mesh axis runs over, the one named last changes fastest.
Arguments:
- jacobian_tiles: bfloat16 [2048, 5, 128, 128], P(('blk', 'sub')), may hold values from -0.25 to 0.25
- column_slots: int32 [2048, 5], P(('blk', 'sub')), may hold values from 0 to 319, as said below
- bus_diagonal: float32 [2048, 128], P(('blk', 'sub')), may hold values from 1 to 4
- bus_residual: float32 [2048, 128], P(('blk', 'sub')), may hold values from -6 to 6
- gen_residual: float32 [65536], P(('blk', 'sub')), may hold values from -6 to 6
- gen_bus: int32 [65536], P(('blk', 'sub')), may hold values from 0 to 8191
- gen_emf: float32 [65536], P(('blk', 'sub')), may hold values from 0.5 to 2
- gen_angle: float32 [65536], P(('blk', 'sub')), may hold values from -3.140625 to 3.140625
- gen_inertia: float32 [65536], P(('blk', 'sub')), may hold values from 0.05 to 0.5
- gen_damping: float32 [65536], P(('blk', 'sub')), may hold values from 0.5 to 4
Outputs:
- delta_bus: float32 [2048, 128], P(('blk', 'sub'))
- delta_gen: float32 [65536], P(('blk', 'sub'))
Inputs may be any that keep to these rules, and one draw needn't show every extreme that they name: `column_slots`: slot 0 of block b names b's own position in its device, b % 64; slot k >= 1 names a value in [k * 64, (k + 1) * 64).
All inputs are finite; a program needn't handle non-finite values.
Results may differ from a plain program's by a relative error of at most 0.00089.
Values may be sent and summed in bfloat16 or wider, within the bound.
A program may use at most 64 MiB of HBM per device.

v0:
```python
import jax
import jax.numpy as jnp
from jax import lax
from jax.sharding import PartitionSpec as P

ITERS = 3


def extended(shard, sides, width):
    for axis, dim in sides:
        peers, length = (lax.axis_size(axis), shard.shape[dim])
        up = [(i, (i + 1) % peers) for i in range(peers)]
        down = [(j, i) for i, j in up]
        last = lax.slice_in_dim(shard, length - width, length, axis=dim)
        first = lax.slice_in_dim(shard, 0, width, axis=dim)
        before = lax.ppermute(last, axis, up)
        after = lax.ppermute(first, axis, down)
        shard = jnp.concatenate([before, shard, after], axis=dim)
    return shard


def small_solve(columns, beta):
    target = [beta] + [jnp.float32(0.0) for _ in columns]
    rotations = []
    upper = []
    for index in range(len(columns)):
        column = list(columns[index])
        for prior in range(len(rotations)):
            cosine, sine = rotations[prior]
            first, second = (column[prior], column[prior + 1])
            column[prior] = cosine * first + sine * second
            column[prior + 1] = -sine * first + cosine * second
        first, second = (column[index], column[index + 1])
        radius = jnp.sqrt(first * first + second * second)
        cosine, sine = (first / radius, second / radius)
        column[index] = radius
        rotations.append((cosine, sine))
        held = target[index]
        target[index] = cosine * held
        target[index + 1] = -sine * held
        upper.append(column[: index + 1])
    count = len(columns)
    answer = [None] * count
    for index in range(count - 1, -1, -1):
        total = target[index]
        for later in range(index + 1, count):
            total = total - upper[later][index] * answer[later]
        answer[index] = total / upper[index][index]
    return answer


def local_inner(first, second):
    return jnp.sum(first[0] * second[0]) + jnp.sum(first[1] * second[1])


def on_device(
    jacobian_tiles,
    column_slots,
    bus_diagonal,
    bus_residual,
    gen_residual,
    gen_bus,
    gen_emf,
    gen_angle,
    gen_inertia,
    gen_damping,
):
    coupling = gen_emf * jnp.cos(gen_angle)
    gen_diag = 10.0 * gen_inertia + gen_damping
    start = (-bus_residual, -gen_residual)
    beta = jnp.sqrt(lax.psum(local_inner(start, start), ("blk", "sub")))
    basis = [(start[0] / beta, start[1] / beta)]
    columns = []
    for index in range(ITERS):
        bus_part = basis[index][0]
        gen_part = basis[index][1]
        rounded = bus_part.astype(jnp.bfloat16)
        along_blk = extended(rounded[None], (("blk", 0),), 1)
        along_sub = extended(rounded[None], (("sub", 0),), 1)
        sources = jnp.concatenate(
            [along_blk[1], along_blk[0], along_blk[2], along_sub[0], along_sub[2]], axis=0
        )
        picked = sources[column_slots]
        product = jnp.einsum(
            "rkij,rkj->ri", jacobian_tiles, picked, preferred_element_type=jnp.float32
        )
        flat = bus_part.reshape(-1)
        back = jax.ops.segment_sum(coupling * gen_part, gen_bus, num_segments=flat.shape[0])
        new_bus = bus_diagonal * bus_part + product - back.reshape(bus_part.shape)
        new_gen = gen_diag * gen_part - coupling * flat[gen_bus]
        work = (new_bus, new_gen)
        column = []
        parts = [local_inner(basis[prior], work) for prior in range(index + 1)]
        parts.append(local_inner(work, work))
        totals = lax.psum(jnp.stack(parts), ("blk", "sub"))
        squared = totals[index + 1]
        for prior in range(index + 1):
            weight = totals[prior]
            column.append(weight)
            squared = squared - weight * weight
            work = (work[0] - weight * basis[prior][0], work[1] - weight * basis[prior][1])
        size_now = jnp.sqrt(squared)
        column.append(size_now)
        columns.append(column)
        basis.append((work[0] / size_now, work[1] / size_now))
    answer = small_solve(columns, beta)
    delta_bus = jnp.zeros_like(bus_residual)
    delta_gen = jnp.zeros_like(gen_residual)
    for index in range(ITERS):
        delta_bus = delta_bus + answer[index] * basis[index][0]
        delta_gen = delta_gen + answer[index] * basis[index][1]
    return (delta_bus, delta_gen)


def solution(mesh):
    in_specs = (
        P(("blk", "sub"), None, None, None),
        P(("blk", "sub"), None),
        P(("blk", "sub"), None),
        P(("blk", "sub"), None),
        P(("blk", "sub")),
        P(("blk", "sub")),
        P(("blk", "sub")),
        P(("blk", "sub")),
        P(("blk", "sub")),
        P(("blk", "sub")),
    )
    out_specs = (P(("blk", "sub"), None), P(("blk", "sub")))
    return jax.shard_map(
        on_device, mesh=mesh, in_specs=in_specs, out_specs=out_specs, check_vma=False
    )
```

profile of v0, /device:TPU:0, one launch (start us, length us, event | category | flops | bytes accessed | tf_op | source)
XLA Modules:
  0.0 323.2 jit_solution(13048021775954051970)
XLA Ops:
  4.6 42.0 %psum.28 = f32[]{:T(128)} all-reduce(f32[]{:T(128)S(6)} %add.105), channel_id=1, replica_groups=mesh['blk'=8,'sub'=4] {'blk','sub'}, use_global_device_ids=true, to_apply=%region_2.0 | all-reduce | flops 1 | bytes 8 | tf_op jit(solution)/shard_map/psum | solution.py:71
  48.1 2.3 collective-permute-start
  50.4 2.4 collective-permute-start.1
  52.9 1.7 collective-permute-start.3
  57.0 11.8 %gather_fusion.1 = f32[2048]{0:T(1024)S(1)} fusion(f32[8192]{0:T(1024)S(1)} %get-tuple-element.33, s32[2048]{0:T(1024)S(1)} %fusion.6), kind=kCustom, calls=%fused_computation.1 | custom fusion | bytes 24576 | tf_op jit(solution)/shard_map/gather | solution.py:90
  68.8 1.4 multiply_reduce_fusion.18
  70.9 11.4 %scatter_custom_fusion = f32[8192]{0:T(1024)S(1)} fusion(s32[2048]{0:T(1024)} %param.15, f32[2048]{0:T(1024)S(1)} %fusion.7, f32[]{:T(128)} %constant.5.clone.1), kind=kCustom, calls=%fused_computation.46 | custom fusion | flops 2048 | bytes 33280 | tf_op jit(solution)/shard_map/scatter-add | solution.py:88
  82.5 1.4 gather_fusion
  83.9 7.3 %fusion.12 = f32[64,1,128,1]{2,1,3,0:T(1,128)S(1)} fusion(bf16[64,5,128,1]{2,3,1,0:T(2,128)(2,1)S(1)} %reshape.119, bf16[64,5,128,128]{3,2,1,0:T(8,128)(2,1)} %param.10), kind=kOutput, calls=%fused_computation.81 | convolution fusion | flops 10485760 | bytes 10600448 | tf_op jit(solution)/shard_map/rkij,rkj->ri/dot_general | solution.py:84
  94.6 38.0 %psum.29 = f32[2]{0:T(128)S(1)} all-reduce(f32[2]{0:T(128)S(1)} %pad_maximum_fusion), channel_id=1, replica_groups=mesh['blk'=8,'sub'=4] {'blk','sub'}, use_global_device_ids=true, to_apply=%region_8.0 | all-reduce | flops 2 | bytes 16 | tf_op jit(solution)/shard_map/psum | solution.py:95
  135.8 2.3 collective-permute-start.4
  138.1 11.8 %gather_fusion.3 = f32[2048]{0:T(1024)S(1)} fusion(f32[8192]{0:T(1024)S(1)} %bitcast.75, s32[2048]{0:T(1024)S(1)} %fusion.6), kind=kCustom, calls=%fused_computation.3 | custom fusion | bytes 24576 | tf_op jit(solution)/shard_map/gather | solution.py:90
  151.3 2.4 collective-permute-start.5
  153.7 1.7 collective-permute-start.7
  156.2 11.4 %scatter_custom_fusion.1 = f32[8192]{0:T(1024)S(1)} fusion(s32[2048]{0:T(1024)} %param.15, f32[2048]{0:T(1024)S(1)} %mul.292, f32[]{:T(128)} %constant.5.clone.1), kind=kCustom, calls=%fused_computation.44 | custom fusion | flops 2048 | bytes 33280 | tf_op jit(solution)/shard_map/scatter-add | solution.py:88
  169.2 7.3 %fusion.13 = f32[64,1,128,1]{2,1,3,0:T(1,128)S(1)} fusion(bf16[64,5,128,1]{2,3,1,0:T(2,128)(2,1)S(1)} %reshape.121, bf16[64,5,128,128]{3,2,1,0:T(8,128)(2,1)} %param.10), kind=kOutput, calls=%fused_computation.82 | convolution fusion | flops 10485760 | bytes 10600448 | tf_op jit(solution)/shard_map/rkij,rkj->ri/dot_general | solution.py:84
  181.1 39.5 %psum.30 = f32[3]{0:T(128)S(1)} all-reduce(f32[3]{0:T(128)S(1)} %pad_maximum_fusion.1), channel_id=1, replica_groups=mesh['blk'=8,'sub'=4] {'blk','sub'}, use_global_device_ids=true, to_apply=%region_16.0 | all-reduce | flops 3 | bytes 24 | tf_op jit(solution)/shard_map/psum | solution.py:95
  225.7 2.3 collective-permute-start.8
  228.1 2.4 collective-permute-start.9
  230.5 1.7 collective-permute-start.11
  232.3 11.8 %gather_fusion.5 = f32[2048]{0:T(1024)S(1)} fusion(f32[8192]{0:T(1024)S(1)} %bitcast.76, s32[2048]{0:T(1024)S(1)} %fusion.6), kind=kCustom, calls=%fused_computation.5 | custom fusion | bytes 24576 | tf_op jit(solution)/shard_map/gather | solution.py:90
  248.7 11.4 %scatter_custom_fusion.2 = f32[8192]{0:T(1024)S(1)} fusion(s32[2048]{0:T(1024)} %param.15, f32[2048]{0:T(1024)S(1)} %get-tuple-element.34, f32[]{:T(128)} %constant.5.clone.1), kind=kCustom, calls=%fused_computation.42 | custom fusion | flops 2048 | bytes 33280 | tf_op jit(solution)/shard_map/scatter-add | solution.py:88
  261.7 7.3 %fusion.14 = f32[64,1,128,1]{2,1,3,0:T(1,128)S(1)} fusion(bf16[64,5,128,1]{2,3,1,0:T(2,128)(2,1)S(1)} %reshape.123, bf16[64,5,128,128]{3,2,1,0:T(8,128)(2,1)} %param.10), kind=kOutput, calls=%fused_computation.83 | convolution fusion | flops 10485760 | bytes 10600448 | tf_op jit(solution)/shard_map/rkij,rkj->ri/dot_general | solution.py:84
  274.9 37.9 %psum.31 = f32[4]{0:T(128)S(1)} all-reduce(f32[4]{0:T(128)S(1)} %pad_maximum_fusion.2), channel_id=1, replica_groups=mesh['blk'=8,'sub'=4] {'blk','sub'}, use_global_device_ids=true, to_apply=%region_26.0 | all-reduce | flops 4 | bytes 32 | tf_op jit(solution)/shard_map/psum | solution.py:95
  (71 shorter events, 20.4 us)
Async XLA Ops:
  48.1 43.2 %copy-start = (f32[64,128]{1,0:T(8,128)S(1)}, f32[64,128]{1,0:T(8,128)}, u32[]{:S(2)}) copy-start(f32[64,128]{1,0:T(8,128)} %param.13) | copy-start | bytes 98308
  48.1 43.2 %copy-start.2 = (f32[64,128]{1,0:T(8,128)S(1)}, f32[64,128]{1,0:T(8,128)}, u32[]{:S(2)}) copy-start(f32[64,128]{1,0:T(8,128)} %param.12) | copy-start | bytes 98308
  48.1 34.3 %collective-permute-start = (bf16[1,64,128]{2,1,0:T(8,128)(2,1)S(1)}, bf16[1,64,128]{2,1,0:T(8,128)(2,1)S(1)}, u32[]{:S(2)}, u32[]{:S(2)}) collective-permute-start(bf16[1,64,128]{2,1,0:T(8,128)(2,1)S(1)} %get-tuple-element.32), channel_id=1, source_target_pairs={{0,4},{4,8},{8,12},{12,16},{16,20},{20,24},{24,28},{28,0},{1,5},{5... | collective-permute-start | bytes 49160 | tf_op jit(solution)/shard_map/ppermute | solution.py:16
  50.4 32.0 %collective-permute-start.1 = (bf16[1,64,128]{2,1,0:T(8,128)(2,1)S(1)}, bf16[1,64,128]{2,1,0:T(8,128)(2,1)S(1)}, u32[]{:S(2)}, u32[]{:S(2)}) collective-permute-start(bf16[1,64,128]{2,1,0:T(8,128)(2,1)S(1)} %get-tuple-element.32), channel_id=1, source_target_pairs={{4,0},{8,4},{12,8},{16,12},{20,16},{24,20},{28,24},{0,28},{5,1},{9... | collective-permute-start | bytes 49160 | tf_op jit(solution)/shard_map/ppermute | solution.py:17
  52.9 29.6 %collective-permute-start.2 = (bf16[1,64,128]{2,1,0:T(8,128)(2,1)S(1)}, bf16[1,64,128]{2,1,0:T(8,128)(2,1)S(1)}, u32[]{:S(2)}, u32[]{:S(2)}) collective-permute-start(bf16[1,64,128]{2,1,0:T(8,128)(2,1)S(1)} %get-tuple-element.32), channel_id=1, source_target_pairs={{0,1},{1,2},{2,3},{3,0},{4,5},{5,6},{6,7},{7,4},{8,9},{9,10},{10,1... | collective-permute-start | bytes 49160 | tf_op jit(solution)/shard_map/ppermute | solution.py:16
  52.9 29.6 %collective-permute-start.3 = (bf16[1,64,128]{2,1,0:T(8,128)(2,1)S(1)}, bf16[1,64,128]{2,1,0:T(8,128)(2,1)S(1)}, u32[]{:S(2)}, u32[]{:S(2)}) collective-permute-start(bf16[1,64,128]{2,1,0:T(8,128)(2,1)S(1)} %get-tuple-element.32), channel_id=1, source_target_pairs={{1,0},{2,1},{3,2},{0,3},{5,4},{6,5},{7,6},{4,7},{9,8},{10,9},{11,1... | collective-permute-start | bytes 49160 | tf_op jit(solution)/shard_map/ppermute | solution.py:17
  82.4 67.5 %copy-start.1 = (f32[2048]{0:T(1024)S(1)}, f32[2048]{0:T(1024)}, u32[]{:S(2)}) copy-start(f32[2048]{0:T(1024)} %param.14) | copy-start | bytes 24580
  82.4 67.5 %copy-start.3 = (f32[2048]{0:T(1024)S(1)}, f32[2048]{0:T(1024)}, u32[]{:S(2)}) copy-start(f32[2048]{0:T(1024)} %param.19) | copy-start | bytes 24580
  82.4 67.5 %copy-start.4 = (f32[2048]{0:T(1024)S(1)}, f32[2048]{0:T(1024)}, u32[]{:S(2)}) copy-start(f32[2048]{0:T(1024)} %param.18) | copy-start | bytes 24580
  135.8 31.9 %collective-permute-start.4 = (bf16[1,64,128]{2,1,0:T(8,128)(2,1)S(1)}, bf16[1,64,128]{2,1,0:T(8,128)(2,1)S(1)}, u32[]{:S(2)}, u32[]{:S(2)}) collective-permute-start(bf16[1,64,128]{2,1,0:T(8,128)(2,1)S(1)} %get-tuple-element.27), channel_id=1, source_target_pairs={{0,4},{4,8},{8,12},{12,16},{16,20},{20,24},{24,28},{28,0},{1,5},{5... | collective-permute-start | bytes 49160 | tf_op jit(solution)/shard_map/ppermute | solution.py:16
  151.3 16.4 %collective-permute-start.5 = (bf16[1,64,128]{2,1,0:T(8,128)(2,1)S(1)}, bf16[1,64,128]{2,1,0:T(8,128)(2,1)S(1)}, u32[]{:S(2)}, u32[]{:S(2)}) collective-permute-start(bf16[1,64,128]{2,1,0:T(8,128)(2,1)S(1)} %get-tuple-element.27), channel_id=1, source_target_pairs={{4,0},{8,4},{12,8},{16,12},{20,16},{24,20},{28,24},{0,28},{5,1},{9... | collective-permute-start | bytes 49160 | tf_op jit(solution)/shard_map/ppermute | solution.py:17
  153.7 14.0 %collective-permute-start.6 = (bf16[1,64,128]{2,1,0:T(8,128)(2,1)S(1)}, bf16[1,64,128]{2,1,0:T(8,128)(2,1)S(1)}, u32[]{:S(2)}, u32[]{:S(2)}) collective-permute-start(bf16[1,64,128]{2,1,0:T(8,128)(2,1)S(1)} %get-tuple-element.27), channel_id=1, source_target_pairs={{0,1},{1,2},{2,3},{3,0},{4,5},{5,6},{6,7},{7,4},{8,9},{9,10},{10,1... | collective-permute-start | bytes 49160 | tf_op jit(solution)/shard_map/ppermute | solution.py:16
  153.7 14.0 %collective-permute-start.7 = (bf16[1,64,128]{2,1,0:T(8,128)(2,1)S(1)}, bf16[1,64,128]{2,1,0:T(8,128)(2,1)S(1)}, u32[]{:S(2)}, u32[]{:S(2)}) collective-permute-start(bf16[1,64,128]{2,1,0:T(8,128)(2,1)S(1)} %get-tuple-element.27), channel_id=1, source_target_pairs={{1,0},{2,1},{3,2},{0,3},{5,4},{6,5},{7,6},{4,7},{9,8},{10,9},{11,1... | collective-permute-start | bytes 49160 | tf_op jit(solution)/shard_map/ppermute | solution.py:17
  225.7 34.4 %collective-permute-start.8 = (bf16[1,64,128]{2,1,0:T(8,128)(2,1)S(1)}, bf16[1,64,128]{2,1,0:T(8,128)(2,1)S(1)}, u32[]{:S(2)}, u32[]{:S(2)}) collective-permute-start(bf16[1,64,128]{2,1,0:T(8,128)(2,1)S(1)} %get-tuple-element.22), channel_id=1, source_target_pairs={{0,4},{4,8},{8,12},{12,16},{16,20},{20,24},{24,28},{28,0},{1,5},{5... | collective-permute-start | bytes 49160 | tf_op jit(solution)/shard_map/ppermute | solution.py:16
  228.1 32.1 %collective-permute-start.9 = (bf16[1,64,128]{2,1,0:T(8,128)(2,1)S(1)}, bf16[1,64,128]{2,1,0:T(8,128)(2,1)S(1)}, u32[]{:S(2)}, u32[]{:S(2)}) collective-permute-start(bf16[1,64,128]{2,1,0:T(8,128)(2,1)S(1)} %get-tuple-element.22), channel_id=1, source_target_pairs={{4,0},{8,4},{12,8},{16,12},{20,16},{24,20},{28,24},{0,28},{5,1},{9... | collective-permute-start | bytes 49160 | tf_op jit(solution)/shard_map/ppermute | solution.py:17
  230.5 29.7 %collective-permute-start.10 = (bf16[1,64,128]{2,1,0:T(8,128)(2,1)S(1)}, bf16[1,64,128]{2,1,0:T(8,128)(2,1)S(1)}, u32[]{:S(2)}, u32[]{:S(2)}) collective-permute-start(bf16[1,64,128]{2,1,0:T(8,128)(2,1)S(1)} %get-tuple-element.22), channel_id=1, source_target_pairs={{0,1},{1,2},{2,3},{3,0},{4,5},{5,6},{6,7},{7,4},{8,9},{9,10},{10,1... | collective-permute-start | bytes 49160 | tf_op jit(solution)/shard_map/ppermute | solution.py:16
  230.5 29.7 %collective-permute-start.11 = (bf16[1,64,128]{2,1,0:T(8,128)(2,1)S(1)}, bf16[1,64,128]{2,1,0:T(8,128)(2,1)S(1)}, u32[]{:S(2)}, u32[]{:S(2)}) collective-permute-start(bf16[1,64,128]{2,1,0:T(8,128)(2,1)S(1)} %get-tuple-element.22), channel_id=1, source_target_pairs={{1,0},{2,1},{3,2},{0,3},{5,4},{6,5},{7,6},{4,7},{9,8},{10,9},{11,1... | collective-permute-start | bytes 49160 | tf_op jit(solution)/shard_map/ppermute | solution.py:17
where the time goes:
time: 325 us; the launch traced here: 323 us
  blocking collectives  157 us (48%)
  other arithmetic  50.8 us (16%)
  local copies, waits for them, and re-layouts  41.9 us (13%)
  between operations  31.5 us (10%)
  matrix products  22 us (7%)
  starting transfers between devices  19.6 us (6%)
    psum x3, blocking collectives, on_device(): totals = lax.psum(jnp.stack(parts), ('blk', 'sub'))  115 us
    psum x1, blocking collectives, on_device(): beta = jnp.sqrt(lax.psum(local_inner(start, start), ('blk', 'sub')))  42 us
    gather x3, local copies, waits for them, and re-layouts, on_device(): new_gen = gen_diag * gen_part - coupling * flat[gen_bus]  35.3 us
    scatter-add x3, other arithmetic, on_device(): jax.ops.segment_sum(coupling * gen_part, gen_bus, num_segments=flat.shape...  34.2 us
    dot_general x3, matrix products, on_device(): jnp.einsum('rkij,rkj->ri', jacobian_tiles, picked, preferred_element_type...  22 us
    ppermute x6, starting transfers between devices, extended(): after = lax.ppermute(first, axis, down)  12.6 us
    reduce_sum x8, other arithmetic, local_inner(): return jnp.sum(first[0] * second[0]) + jnp.sum(first[1] * second[1])  8.26 us
    ppermute x6, starting transfers between devices, extended(): before = lax.ppermute(last, axis, up)  6.99 us
  transfers between devices with their start and end apart: 12, of which 0 were waited for; matrix products, arithmetic and copies ran while one was open for 24% of the time, Pallas kernels for 0%

commit v1 on v0

v1 whole, which is shorter than its diff:
```python
import functools

import jax
import jax.numpy as jnp
from jax import lax
from jax.experimental import pallas as pl
from jax.experimental.pallas import tpu as pltpu
from jax.sharding import PartitionSpec as P

ITERS = 3
MESH = pl.DeviceIdType.MESH
NT = (((1,), (1,)), ((), ()))
F32 = jnp.float32
BF16 = jnp.bfloat16


def small_solve(columns, beta):
    target = [beta] + [jnp.zeros_like(beta) for _ in columns]
    rotations = []
    upper = []
    for index in range(len(columns)):
        column = list(columns[index])
        for prior in range(len(rotations)):
            cosine, sine = rotations[prior]
            first, second = (column[prior], column[prior + 1])
            column[prior] = cosine * first + sine * second
            column[prior + 1] = -sine * first + cosine * second
        first, second = (column[index], column[index + 1])
        radius = jnp.sqrt(first * first + second * second)
        cosine, sine = (first / radius, second / radius)
        column[index] = radius
        rotations.append((cosine, sine))
        held = target[index]
        target[index] = cosine * held
        target[index + 1] = -sine * held
        upper.append(column[: index + 1])
    count = len(columns)
    answer = [None] * count
    for index in range(count - 1, -1, -1):
        total = target[index]
        for later in range(index + 1, count):
            total = total - upper[later][index] * answer[later]
        answer[index] = total / upper[index][index]
    return answer


def halves(value):
    high = value.astype(BF16).astype(F32)
    return high, value - high


def fold(value):
    total = value[0:8]
    for at in range(8, value.shape[0], 8):
        total = total + value[at : at + 8]
    return total


def kernel(
    n_blk,
    n_sub,
    slots_ref,
    tiles_ref,
    diag_ref,
    bus_res_ref,
    gen_res_ref,
    gen_bus_ref,
    emf_ref,
    angle_ref,
    inertia_ref,
    damping_ref,
    out_bus_ref,
    out_gen_ref,
    own_tiles,
    far_tiles,
    sources_0,
    sources_1,
    sources_2,
    picked,
    product,
    row_hot,
    lane_hot,
    spread,
    fetched,
    sum_sub,
    sum_blk,
    own_sem,
    far_sem,
    halo_send,
    halo_recv,
    sub_send,
    sub_recv,
    blk_send,
    blk_recv,
):
    rows, tile = diag_ref.shape
    n_slots = tiles_ref.shape[1]
    groups = rows // 8
    chunks = gen_bus_ref.shape[0]
    sources = (sources_0, sources_1, sources_2)
    blk, sub = lax.axis_index("blk"), lax.axis_index("sub")

    def near(blk_step, sub_step):
        return (
            lax.rem(blk + blk_step + n_blk, n_blk),
            lax.rem(sub + sub_step + n_sub, n_sub),
        )

    def own_copy(g):
        part = pl.ds(g * 8, 8)
        return pltpu.make_async_copy(tiles_ref.at[part, 0], own_tiles.at[part], own_sem.at[g])

    def far_copy(g, k):
        part = pl.ds(g * 8, 8)
        return pltpu.make_async_copy(
            tiles_ref.at[part, k],
            far_tiles.at[part, :, pl.ds((k - 1) * tile, tile)],
            far_sem.at[g, k - 1],
        )

    for g in range(groups):
        own_copy(g).start()
    for g in range(groups):
        for k in range(1, n_slots):
            far_copy(g, k).start()

    barrier = pltpu.get_barrier_semaphore()
    for step in range(1, n_sub):
        pl.semaphore_signal(barrier, inc=1, device_id=near(0, step), device_id_type=MESH)
    for step in range(1, n_blk):
        pl.semaphore_signal(barrier, inc=1, device_id=near(step, 0), device_id_type=MESH)

    sends = []

    def send_halo(at, value):
        sources[at][0:rows, :] = value
        copies = []
        for region, device in enumerate((near(1, 0), near(-1, 0), near(0, 1), near(0, -1))):
            copy = pltpu.make_async_remote_copy(
                src_ref=sources[at].at[pl.ds(0, rows)],
                dst_ref=sources[at].at[pl.ds((region + 1) * rows, rows)],
                send_sem=halo_send.at[at, region],
                recv_sem=halo_recv.at[at, region],
                device_id=device,
                device_id_type=MESH,
            )
            copy.start()
            copies.append(copy)
        sends.extend(copies)
        return copies

    def send_sums(buffer, at, send_sem, recv_sem, count, device_at):
        copies = []
        for step in range(1, count):
            copy = pltpu.make_async_remote_copy(
                src_ref=buffer.at[at, 0],
                dst_ref=buffer.at[at, step],
                send_sem=send_sem.at[at, step],
                recv_sem=recv_sem.at[at, step],
                device_id=device_at(step),
                device_id_type=MESH,
            )
            copy.start()
            copies.append(copy)
        sends.extend(copies)
        return copies

    def start_sums(at, pairs):
        for index, (first, second) in enumerate(pairs):
            total = fold(first[0] * second[0]) + fold(first[1] * second[1])
            sum_sub[at, 0, index : index + 1, :] = jnp.sum(total, axis=0, keepdims=True)
        for index in range(len(pairs), 8):
            sum_sub[at, 0, index : index + 1, :] = jnp.zeros((1, tile), F32)
        return send_sums(sum_sub, at, sub_send, sub_recv, n_sub, lambda step: near(0, step))

    def pass_sums(at, copies):
        for copy in copies:
            copy.wait_recv()
        sum_blk[at, 0] = jnp.sum(sum_sub[at], axis=0)
        return send_sums(sum_blk, at, blk_send, blk_recv, n_blk, lambda step: near(step, 0))

    def finish_sums(at, copies, count):
        for copy in copies:
            copy.wait_recv()
        totals = jnp.sum(jnp.sum(sum_blk[at], axis=0), axis=1, keepdims=True)
        return [totals[index : index + 1, :] for index in range(count)]

    bus0 = -bus_res_ref[...]
    gen0 = -gen_res_ref[...]
    pl.semaphore_wait(barrier, n_sub + n_blk - 2)
    halo = send_halo(0, bus0)

    coupling = emf_ref[...] * jnp.cos(angle_ref[...])
    gen_diag = 10.0 * inertia_ref[...] + damping_ref[...]
    at_bus = gen_bus_ref[...]
    bus_row, bus_lane = at_bus // tile, at_bus % tile
    ids = lax.broadcasted_iota(jnp.int32, (2 * rows, tile), 0)
    upper_half = ids < rows
    row_ids = jnp.where(upper_half, ids, ids - rows)
    lane_ids = lax.broadcasted_iota(jnp.int32, (tile, tile), 0)
    for i in range(chunks):
        span = slice(i * tile, (i + 1) * tile)
        row_hot[:, span] = jnp.where(row_ids == bus_row[i : i + 1, :], 1.0, 0.0).astype(BF16)
        lane_hot[:, span] = jnp.where(lane_ids == bus_lane[i : i + 1, :], 1.0, 0.0).astype(BF16)

    pick_row = lax.broadcasted_iota(jnp.int32, (8, tile), 0)

    def diagonal_blocks(result):
        total = jnp.zeros((8, tile), F32)
        for q in range(8):
            span = slice(q * tile, (q + 1) * tile)
            total = jnp.where(pick_row == q, result[0:8, span] + result[8:16, span], total)
        return total

    def generators(vector):
        bus, gen = vector
        high, low = halves(bus)
        stacked = jnp.concatenate([high, low], axis=0).T.astype(BF16)
        weighted = coupling * gen
        w_high, w_low = halves(weighted)
        for i in range(chunks):
            span = slice(i * tile, (i + 1) * tile)
            by_lane = jnp.dot(stacked, row_hot[:, span], preferred_element_type=F32)
            fetched[i : i + 1, :] = jnp.sum(
                by_lane * lane_hot[:, span].astype(F32), axis=0, keepdims=True
            )
            both = jnp.where(upper_half, w_high[i : i + 1, :], w_low[i : i + 1, :])
            spread[:, span] = (row_hot[:, span].astype(F32) * both).astype(BF16)
        back = lax.dot_general(spread[...], lane_hot[...], NT, preferred_element_type=F32)
        new_bus = diag_ref[...] * bus - (back[0:rows] + back[rows : 2 * rows])
        new_gen = gen_diag * gen - coupling * fetched[...]
        return new_bus, new_gen

    def apply(at, vector, halo, meanwhile):
        new_bus, new_gen = generators(vector)
        product[...] = new_bus

        def own_step(g, carry):
            part = pl.ds(pl.multiple_of(g * 8, 8), 8)
            if at == 0:
                own_copy(g).wait()
            left = jnp.concatenate(halves(sources[at][part, :]), axis=0).astype(BF16)
            right = own_tiles[part].reshape(8 * tile, tile)
            result = lax.dot_general(left, right, NT, preferred_element_type=F32)
            product[part, :] += diagonal_blocks(result)
            return carry

        lax.fori_loop(0, groups, own_step, 0)
        later = meanwhile() if meanwhile else None
        for copy in halo:
            copy.wait_recv()

        def far_step(g, carry):
            part = pl.ds(pl.multiple_of(g * 8, 8), 8)
            for q in range(8):
                for k in range(1, n_slots):
                    row = sources[at][pl.ds(slots_ref[k, g * 8 + q], 1), :]
                    picked[g, q : q + 1, (k - 1) * tile : k * tile] = row
            if at == 0:
                for k in range(1, n_slots):
                    far_copy(g, k).wait()
            left = jnp.concatenate(halves(picked[g]), axis=0).astype(BF16)
            right = far_tiles[part].reshape(8 * tile, (n_slots - 1) * tile)
            result = lax.dot_general(left, right, NT, preferred_element_type=F32)
            product[part, :] += diagonal_blocks(result)
            return carry

        lax.fori_loop(0, groups, far_step, 0)
        return (product[...], new_gen), later

    def combine(terms):
        return tuple(
            functools.reduce(lambda a, b: a + b, [weight * pair[part] for weight, pair in terms])
            for part in (0, 1)
        )

    start = (bus0, gen0)
    first, _ = apply(0, start, halo, None)
    halo = send_halo(1, first[0])
    sums = start_sums(0, [(start, start), (start, first), (first, first)])
    second, later = apply(1, first, halo, lambda: pass_sums(0, sums))
    norm2, cross, size2 = finish_sums(0, later, 3)
    beta = jnp.sqrt(norm2)
    inv_beta = 1.0 / beta
    inv_norm2 = inv_beta * inv_beta
    h00 = cross * inv_norm2
    h10 = jnp.sqrt(size2 * inv_norm2 - h00 * h00)
    inv = 1.0 / h10
    v0 = combine([(inv_beta, start)])
    w0 = combine([(inv_beta, first)])
    v1 = combine([(inv, w0), (-inv * h00, v0)])
    w1 = combine([(inv * inv_beta, second), (-inv * h00, w0)])

    halo = send_halo(2, w1[0])
    sums = start_sums(1, [(v0, w1), (v1, w1), (w1, w1)])
    third, later = apply(2, w1, halo, lambda: pass_sums(1, sums))
    h01, h11, size2 = finish_sums(1, later, 3)
    h21 = jnp.sqrt(size2 - h01 * h01 - h11 * h11)
    inv = 1.0 / h21
    v2 = combine([(inv, w1), (-inv * h01, v0), (-inv * h11, v1)])
    w2 = combine([(inv, third), (-inv * h01, w0), (-inv * h11, w1)])

    sums = start_sums(2, [(v0, w2), (v1, w2), (v2, w2), (w2, w2)])
    later = pass_sums(2, sums)
    h02, h12, h22, size2 = finish_sums(2, later, 4)
    h32 = jnp.sqrt(size2 - h02 * h02 - h12 * h12 - h22 * h22)

    answer = small_solve([[h00, h10], [h01, h11, h21], [h02, h12, h22, h32]], beta)
    out_bus_ref[...], out_gen_ref[...] = combine(list(zip(answer, (v0, v1, v2))))
    for copy in sends:
        copy.wait_send()


def on_device(
    n_blk,
    n_sub,
    jacobian_tiles,
    column_slots,
    bus_diagonal,
    bus_residual,
    gen_residual,
    gen_bus,
    gen_emf,
    gen_angle,
    gen_inertia,
    gen_damping,
):
    rows, n_slots, tile, _ = jacobian_tiles.shape
    gens = gen_bus.shape[0]
    chunks = gens // tile
    groups = rows // 8
    far = n_slots - 1
    generator = [
        part.reshape(chunks, tile)
        for part in (gen_residual, gen_bus, gen_emf, gen_angle, gen_inertia, gen_damping)
    ]
    vmem = pl.BlockSpec(memory_space=pltpu.VMEM)
    dma = pltpu.SemaphoreType.DMA
    delta_bus, delta_gen = pl.pallas_call(
        functools.partial(kernel, n_blk, n_sub),
        out_shape=(
            jax.ShapeDtypeStruct((rows, tile), F32),
            jax.ShapeDtypeStruct((chunks, tile), F32),
        ),
        in_specs=[pl.BlockSpec(memory_space=pltpu.SMEM), pl.BlockSpec(memory_space=pl.ANY)]
        + [vmem] * 8,
        out_specs=(vmem, vmem),
        scratch_shapes=[
            pltpu.VMEM((rows, tile, tile), BF16),
            pltpu.VMEM((rows, tile, far * tile), BF16),
            *[pltpu.VMEM((n_slots * rows, tile), F32)] * ITERS,
            pltpu.VMEM((groups, 8, far * tile), F32),
            pltpu.VMEM((rows, tile), F32),
            pltpu.VMEM((2 * rows, gens), BF16),
            pltpu.VMEM((tile, gens), BF16),
            pltpu.VMEM((2 * rows, gens), BF16),
            pltpu.VMEM((chunks, tile), F32),
            pltpu.VMEM((ITERS, n_sub, 8, tile), F32),
            pltpu.VMEM((ITERS, n_blk, 8, tile), F32),
            dma((groups,)),
            dma((groups, far)),
            dma((ITERS, 4)),
            dma((ITERS, 4)),
            dma((ITERS, n_sub)),
            dma((ITERS, n_sub)),
            dma((ITERS, n_blk)),
            dma((ITERS, n_blk)),
        ],
        compiler_params=pltpu.CompilerParams(
            collective_id=0, has_side_effects=True, vmem_limit_bytes=48 * 1024 * 1024
        ),
    )(column_slots.T, jacobian_tiles, bus_diagonal, bus_residual, *generator)
    return delta_bus, delta_gen.reshape(gens)


def solution(mesh):
    both = ("blk", "sub")
    in_specs = (
        P(both, None, None, None),
        P(both, None),
        P(both, None),
        P(both, None),
        P(both),
        P(both),
        P(both),
        P(both),
        P(both),
        P(both),
    )
    return jax.shard_map(
        functools.partial(on_device, mesh.shape["blk"], mesh.shape["sub"]),
        mesh=mesh,
        in_specs=in_specs,
        out_specs=(P(both, None), P(both)),
        check_vma=False,
    )
```

time: 325 us -> 47.1 us (0.14)
  blocking collectives: 157 us -> 0 us
  other arithmetic: 50.8 us -> 0 us
  Pallas kernels: 0 us -> 38.3 us
  local copies, waits for them, and re-layouts: 41.9 us -> 7.59 us
  between operations: 31.5 us -> 0.66 us
  matrix products: 22 us -> 0 us
  starting transfers between devices: 19.6 us -> 0 us
    psum x4 -> x0, blocking collectives: 157 us -> none  [the longest x3 115 us: on_device(): totals = lax.psum(jnp.stack(parts), ('blk', 'sub'))]
    gather x9 -> x0, local copies, waits for them, and re-layouts: 39.6 us -> none  [the longest x3 35.3 us: on_device(): new_gen = gen_diag * gen_part - coupling * flat[gen_bus]]
    pallas_call x0 -> x1, Pallas kernels: none -> 38.3 us  [on_device(): pl.pallas_call(functools.partial(kernel, n_blk, n_sub), out_shape=(jax.Sh...]
    scatter-add x3 -> x0, other arithmetic: 34.2 us -> none  [on_device(): jax.ops.segment_sum(coupling * gen_part, gen_bus, num_segments=flat.shape...]
    dot_general x3 -> x0, matrix products: 22 us -> none  [on_device(): jnp.einsum('rkij,rkj->ri', jacobian_tiles, picked, preferred_element_type...]
    ppermute x12 -> x0, starting transfers between devices: 19.6 us -> none  [the longest x6 12.6 us: extended(): after = lax.ppermute(first, axis, down)]
    reduce_sum x8 -> x0, other arithmetic: 8.26 us -> none  [local_inner(): return jnp.sum(first[0] * second[0]) + jnp.sum(first[1] * second[1])]
    unnamed x19 -> x20, local copies, waits for them, and re-layouts: 0.11 us -> 7.59 us
  transfers between devices with their start and end apart: 12 -> 0, of which waited for: 0 -> 0; matrix products, arithmetic and copies ran while one was open for 24% -> 0% of each run, Pallas kernels for 0% -> 0%
where the time goes in v1:
time: 47.1 us; the launch traced here: 46.5 us
  Pallas kernels  38.3 us (81%)
  local copies, waits for them, and re-layouts  7.59 us (16%)
  between operations  0.66 us (1%)
    pallas_call x1, Pallas kernels, on_device(): pl.pallas_call(functools.partial(kernel, n_blk, n_sub), out_shape=(jax.Sh...  38.3 us
    unnamed x20, local copies, waits for them, and re-layouts  7.59 us

profile of v1, /device:TPU:0, one launch (start us, length us, event | category | flops | bytes accessed | tf_op | source)
XLA Modules:
  0.0 46.5 jit_solution(14318494813494085164)
XLA Ops:
  0.6 0.0 copy-start
  0.6 0.7 %copy-done = f32[64,128]{1,0:T(8,128)S(1)} copy-done((f32[64,128]{1,0:T(8,128)S(1)}, f32[64,128]{1,0:T(8,128)}, u32[]{:S(2)}) %copy-start) | copy-done | bytes 32792
  1.4 0.0 copy-start.1
  1.4 0.8 %copy-done.1 = f32[64,128]{1,0:T(8,128)S(1)} copy-done((f32[64,128]{1,0:T(8,128)S(1)}, f32[64,128]{1,0:T(8,128)}, u32[]{:S(2)}) %copy-start.1) | copy-done | bytes 32792
  2.2 0.0 copy-start.2
  2.2 0.7 %copy-done.2 = f32[2048]{0:T(1024)S(1)} copy-done((f32[2048]{0:T(1024)S(1)}, f32[2048]{0:T(1024)}, u32[]{:S(2)}) %copy-start.2) | copy-done | bytes 8216
  2.8 0.0 copy-start.3
  2.9 0.7 %copy-done.3 = s32[2048]{0:T(1024)S(1)} copy-done((s32[2048]{0:T(1024)S(1)}, s32[2048]{0:T(1024)}, u32[]{:S(2)}) %copy-start.3) | copy-done | bytes 8216
  3.5 0.0 copy-start.4
  3.5 0.7 %copy-done.4 = f32[2048]{0:T(1024)S(1)} copy-done((f32[2048]{0:T(1024)S(1)}, f32[2048]{0:T(1024)}, u32[]{:S(2)}) %copy-start.4) | copy-done | bytes 8216
  4.2 0.0 copy-start.5
  4.2 0.7 %copy-done.5 = f32[2048]{0:T(1024)S(1)} copy-done((f32[2048]{0:T(1024)S(1)}, f32[2048]{0:T(1024)}, u32[]{:S(2)}) %copy-start.5) | copy-done | bytes 8216
  4.9 0.0 copy-start.6
  4.9 0.7 %copy-done.6 = f32[2048]{0:T(1024)S(1)} copy-done((f32[2048]{0:T(1024)S(1)}, f32[2048]{0:T(1024)}, u32[]{:S(2)}) %copy-start.6) | copy-done | bytes 8216
  5.6 0.0 copy-start.7
  5.6 0.7 %copy-done.7 = f32[2048]{0:T(1024)S(1)} copy-done((f32[2048]{0:T(1024)S(1)}, f32[2048]{0:T(1024)}, u32[]{:S(2)}) %copy-start.7) | copy-done | bytes 8216
  6.3 0.0 copy-start.8
  6.3 0.7 %copy-done.8 = s32[64,5]{0,1:T(8,128)S(1)} copy-done((s32[64,5]{0,1:T(8,128)S(1)}, s32[64,5]{0,1:T(8,128)}, u32[]{:S(2)}) %copy-start.8) | copy-done | bytes 1304
  7.0 38.3 %shard_map.113 = (f32[64,128]{1,0:T(8,128)S(1)}, f32[16,128]{1,0:T(8,128)S(1)}) custom-call(s32[5,64]{1,0:T(8,128)S(1)} %bitcast.15, bf16[64,5,128,128]{3,2,1,0:T(8,128)(2,1)} %tiles_ref.1, f32[64,128]{1,0:T(8,128)S(1)} %copy-done, f32[64,128]{1,0:T(8,128)S(1)} %copy-done.1, f32[16,128]{1,0:T(8,128)S(1)} %bitcast.8, s32[16,128]{1,0:T(8,128)S(1)} %bitcast.9, ...), custom_call_target="tpu_custom_call" | custom-call | tf_op jit(solution)/shard_map/pallas_call | solution.py:339
  45.3 0.6 %copy.14 = f32[64,128]{1,0:T(8,128)} copy(f32[64,128]{1,0:T(8,128)S(1)} %get-tuple-element.8) | data formatting | bytes 65536
  45.9 0.6 %copy.15 = f32[2048]{0:T(1024)} copy(f32[2048]{0:T(1024)S(1)} %bitcast.14) | data formatting | bytes 16384
Async XLA Ops:
  0.6 0.8 %copy-start = (f32[64,128]{1,0:T(8,128)S(1)}, f32[64,128]{1,0:T(8,128)}, u32[]{:S(2)}) copy-start(f32[64,128]{1,0:T(8,128)} %diag_ref.1) | copy-start | bytes 98308
  1.4 0.8 %copy-start.1 = (f32[64,128]{1,0:T(8,128)S(1)}, f32[64,128]{1,0:T(8,128)}, u32[]{:S(2)}) copy-start(f32[64,128]{1,0:T(8,128)} %bus_res_ref.1) | copy-start | bytes 98308
  2.2 0.7 %copy-start.2 = (f32[2048]{0:T(1024)S(1)}, f32[2048]{0:T(1024)}, u32[]{:S(2)}) copy-start(f32[2048]{0:T(1024)} %param.14) | copy-start | bytes 24580
  2.8 0.7 %copy-start.3 = (s32[2048]{0:T(1024)S(1)}, s32[2048]{0:T(1024)}, u32[]{:S(2)}) copy-start(s32[2048]{0:T(1024)} %param.15) | copy-start | bytes 24580
  3.5 0.7 %copy-start.4 = (f32[2048]{0:T(1024)S(1)}, f32[2048]{0:T(1024)}, u32[]{:S(2)}) copy-start(f32[2048]{0:T(1024)} %param.16) | copy-start | bytes 24580
  4.2 0.7 %copy-start.5 = (f32[2048]{0:T(1024)S(1)}, f32[2048]{0:T(1024)}, u32[]{:S(2)}) copy-start(f32[2048]{0:T(1024)} %param.17) | copy-start | bytes 24580
  4.9 0.7 %copy-start.6 = (f32[2048]{0:T(1024)S(1)}, f32[2048]{0:T(1024)}, u32[]{:S(2)}) copy-start(f32[2048]{0:T(1024)} %param.18) | copy-start | bytes 24580
  5.6 0.7 %copy-start.7 = (f32[2048]{0:T(1024)S(1)}, f32[2048]{0:T(1024)}, u32[]{:S(2)}) copy-start(f32[2048]{0:T(1024)} %param.19) | copy-start | bytes 24580
  6.3 0.7 %copy-start.8 = (s32[64,5]{0,1:T(8,128)S(1)}, s32[64,5]{0,1:T(8,128)}, u32[]{:S(2)}) copy-start(s32[64,5]{0,1:T(8,128)} %param.11) | copy-start | bytes 3844

commit v2 on v1

--- a/solution.py
+++ b/solution.py
@@ -56,43 +56,50 @@
     return total
 
 
-def kernel(
-    n_blk,
-    n_sub,
-    slots_ref,
-    tiles_ref,
-    diag_ref,
-    bus_res_ref,
-    gen_res_ref,
-    gen_bus_ref,
-    emf_ref,
-    angle_ref,
-    inertia_ref,
-    damping_ref,
-    out_bus_ref,
-    out_gen_ref,
-    own_tiles,
-    far_tiles,
-    sources_0,
-    sources_1,
-    sources_2,
-    picked,
-    product,
-    row_hot,
-    lane_hot,
-    spread,
-    fetched,
-    sum_sub,
-    sum_blk,
-    own_sem,
-    far_sem,
-    halo_send,
-    halo_recv,
-    sub_send,
-    sub_recv,
-    blk_send,
-    blk_recv,
-):
+def kernel(n_blk, n_sub, tiles_ref, *refs):
+    in_hbm, refs = refs[:9], refs[9:]
+    out_bus_ref, out_gen_ref = refs[:2]
+    in_place, small_sem = refs[2:11], refs[11]
+    (
+        own_tiles,
+        far_tiles,
+        sources_0,
+        sources_1,
+        sources_2,
+        picked,
+        product,
+        row_hot,
+        lane_hot,
+        spread,
+        fetched,
+        sum_sub,
+        sum_blk,
+        own_sem,
+        far_sem,
+        halo_send,
+        halo_recv,
+        sub_send,
+        sub_recv,
+        blk_send,
+        blk_recv,
+    ) = refs[12:]
+    (
+        bus_res_ref,
+        gen_res_ref,
+        gen_bus_ref,
+        emf_ref,
+        angle_ref,
+        inertia_ref,
+        damping_ref,
+        diag_ref,
+        slots_ref,
+    ) = in_place
+    small = [
+        pltpu.make_async_copy(here, there, small_sem.at[index])
+        for index, (here, there) in enumerate(zip(in_hbm, in_place))
+    ]
+    for copy in small:
+        copy.start()
     rows, tile = diag_ref.shape
     n_slots = tiles_ref.shape[1]
     groups = rows // 8
@@ -185,6 +192,8 @@
         totals = jnp.sum(jnp.sum(sum_blk[at], axis=0), axis=1, keepdims=True)
         return [totals[index : index + 1, :] for index in range(count)]
 
+    for copy in small:
+        copy.wait()
     bus0 = -bus_res_ref[...]
     gen0 = -gen_res_ref[...]
     pl.semaphore_wait(barrier, n_sub + n_blk - 2)
@@ -342,10 +351,16 @@
             jax.ShapeDtypeStruct((rows, tile), F32),
             jax.ShapeDtypeStruct((chunks, tile), F32),
         ),
-        in_specs=[pl.BlockSpec(memory_space=pltpu.SMEM), pl.BlockSpec(memory_space=pl.ANY)]
-        + [vmem] * 8,
+        in_specs=[pl.BlockSpec(memory_space=pltpu.HBM)] * 10,
         out_specs=(vmem, vmem),
         scratch_shapes=[
+            pltpu.VMEM((rows, tile), F32),
+            pltpu.VMEM((chunks, tile), F32),
+            pltpu.VMEM((chunks, tile), jnp.int32),
+            *[pltpu.VMEM((chunks, tile), F32)] * 4,
+            pltpu.VMEM((rows, tile), F32),
+            pltpu.SMEM((n_slots, rows), jnp.int32),
+            dma((9,)),
             pltpu.VMEM((rows, tile, tile), BF16),
             pltpu.VMEM((rows, tile, far * tile), BF16),
             *[pltpu.VMEM((n_slots * rows, tile), F32)] * ITERS,
@@ -367,9 +382,9 @@
             dma((ITERS, n_blk)),
         ],
         compiler_params=pltpu.CompilerParams(
-            collective_id=0, has_side_effects=True, vmem_limit_bytes=48 * 1024 * 1024
+            collective_id=0, has_side_effects=True, vmem_limit_bytes=60 * 1024 * 1024
         ),
-    )(column_slots.T, jacobian_tiles, bus_diagonal, bus_residual, *generator)
+    )(jacobian_tiles, bus_residual, *generator, bus_diagonal, column_slots.T)
     return delta_bus, delta_gen.reshape(gens)
 
 

time: 47.1 us -> 42 us (0.89)
  local copies, waits for them, and re-layouts: 7.59 us -> 2.67 us
    unnamed x20 -> x2, local copies, waits for them, and re-layouts: 7.59 us -> 2.67 us
where the time goes in v2:
time: 42 us; the launch traced here: 41.7 us
  Pallas kernels  38.4 us (91%)
  local copies, waits for them, and re-layouts  2.67 us (6%)
  between operations  0.64 us (2%)
    pallas_call x1, Pallas kernels, on_device(): pl.pallas_call(functools.partial(kernel, n_blk, n_sub), out_shape=(jax.Sh...  38.4 us
    unnamed x2, local copies, waits for them, and re-layouts  2.67 us

profile of v2, /device:TPU:0, one launch (start us, length us, event | category | flops | bytes accessed | tf_op | source)
XLA Modules:
  0.0 41.7 jit_solution(7442423870492767922)
XLA Ops:
  0.6 38.4 %shard_map.113 = (f32[64,128]{1,0:T(8,128)}, f32[16,128]{1,0:T(8,128)}) custom-call(bf16[64,5,128,128]{3,2,1,0:T(8,128)(2,1)} %tiles_ref.1, f32[64,128]{1,0:T(8,128)} %refs_0_.1, f32[16,128]{1,0:T(8,128)} %bitcast.8, s32[16,128]{1,0:T(8,128)} %bitcast.9, f32[16,128]{1,0:T(8,128)} %bitcast.10, f32[16,128]{1,0:T(8,128)} %bitcast.11, f32[16,128]{1,0:T(8,128)} %bitcast.12, ...), custom_call_target="tpu_custom_call" | custom-call | tf_op jit(solution)/shard_map/pallas_call | solution.py:348
  39.1 1.4 %copy.14 = f32[64,128]{1,0:T(8,128)} copy(f32[64,128]{1,0:T(8,128)} %get-tuple-element.8) | data formatting | bytes 65536
  40.4 1.3 %copy.15 = f32[2048]{0:T(1024)} copy(f32[2048]{0:T(1024)} %bitcast.14) | data formatting | bytes 16384

commit v3 on v2

--- a/solution.py
+++ b/solution.py
@@ -103,6 +103,7 @@
     rows, tile = diag_ref.shape
     n_slots = tiles_ref.shape[1]
     groups = rows // 8
+    half = groups // 2
     chunks = gen_bus_ref.shape[0]
     sources = (sources_0, sources_1, sources_2)
     blk, sub = lax.axis_index("blk"), lax.axis_index("sub")
@@ -115,7 +116,10 @@
 
     def own_copy(g):
         part = pl.ds(g * 8, 8)
-        return pltpu.make_async_copy(tiles_ref.at[part, 0], own_tiles.at[part], own_sem.at[g])
+        there = own_tiles.at[
+            pl.ds(g % half * 8, 8), :, pl.ds(pl.multiple_of(g // half * tile, tile), tile)
+        ]
+        return pltpu.make_async_copy(tiles_ref.at[part, 0], there, own_sem.at[g])
 
     def far_copy(g, k):
         part = pl.ds(g * 8, 8)
@@ -246,15 +250,27 @@
 
         def own_step(g, carry):
             part = pl.ds(pl.multiple_of(g * 8, 8), 8)
+            other = pl.ds(pl.multiple_of((g + half) * 8, 8), 8)
             if at == 0:
                 own_copy(g).wait()
-            left = jnp.concatenate(halves(sources[at][part, :]), axis=0).astype(BF16)
-            right = own_tiles[part].reshape(8 * tile, tile)
+                own_copy(g + half).wait()
+            first = jnp.concatenate(halves(sources[at][part, :]), axis=0)
+            second = jnp.concatenate(halves(sources[at][other, :]), axis=0)
+            none = jnp.zeros_like(first)
+            left = jnp.concatenate(
+                [
+                    jnp.concatenate([first, none], axis=1),
+                    jnp.concatenate([none, second], axis=1),
+                ],
+                axis=0,
+            ).astype(BF16)
+            right = own_tiles[part].reshape(8 * tile, 2 * tile)
             result = lax.dot_general(left, right, NT, preferred_element_type=F32)
-            product[part, :] += diagonal_blocks(result)
+            product[part, :] += diagonal_blocks(result[0:16])
+            product[other, :] += diagonal_blocks(result[16:32])
             return carry
 
-        lax.fori_loop(0, groups, own_step, 0)
+        lax.fori_loop(0, half, own_step, 0)
         later = meanwhile() if meanwhile else None
         for copy in halo:
             copy.wait_recv()
@@ -361,7 +377,7 @@
             pltpu.VMEM((rows, tile), F32),
             pltpu.SMEM((n_slots, rows), jnp.int32),
             dma((9,)),
-            pltpu.VMEM((rows, tile, tile), BF16),
+            pltpu.VMEM((rows // 2, tile, 2 * tile), BF16),
             pltpu.VMEM((rows, tile, far * tile), BF16),
             *[pltpu.VMEM((n_slots * rows, tile), F32)] * ITERS,
             pltpu.VMEM((groups, 8, far * tile), F32),

time: 42 us -> 42 us (level)
  no operation moved by 1% of the time
where the time goes in v3:
time: 42 us; the launch traced here: 41.8 us
  Pallas kernels  38.4 us (91%)
  local copies, waits for them, and re-layouts  2.67 us (6%)
  between operations  0.64 us (2%)
    pallas_call x1, Pallas kernels, on_device(): pl.pallas_call(functools.partial(kernel, n_blk, n_sub), out_shape=(jax.Sh...  38.4 us
    unnamed x2, local copies, waits for them, and re-layouts  2.67 us

profile of v3, /device:TPU:0, one launch (start us, length us, event | category | flops | bytes accessed | tf_op | source)
XLA Modules:
  0.0 41.8 jit_solution(12062741227194698059)
XLA Ops:
  0.6 38.4 %shard_map.113 = (f32[64,128]{1,0:T(8,128)}, f32[16,128]{1,0:T(8,128)}) custom-call(bf16[64,5,128,128]{3,2,1,0:T(8,128)(2,1)} %tiles_ref.1, f32[64,128]{1,0:T(8,128)} %refs_0_.1, f32[16,128]{1,0:T(8,128)} %bitcast.8, s32[16,128]{1,0:T(8,128)} %bitcast.9, f32[16,128]{1,0:T(8,128)} %bitcast.10, f32[16,128]{1,0:T(8,128)} %bitcast.11, f32[16,128]{1,0:T(8,128)} %bitcast.12, ...), custom_call_target="tpu_custom_call" | custom-call | tf_op jit(solution)/shard_map/pallas_call | solution.py:364
  39.1 1.4 %copy.14 = f32[64,128]{1,0:T(8,128)} copy(f32[64,128]{1,0:T(8,128)} %get-tuple-element.8) | data formatting | bytes 65536
  40.5 1.3 %copy.15 = f32[2048]{0:T(1024)} copy(f32[2048]{0:T(1024)} %bitcast.14) | data formatting | bytes 16384
